TPU v7x, 128 devices: a whole 4x4x4 slice. The times are simulated.
128 devices in a mesh: blk: 32 (over x, y, z_lo), rep: 4 (over z_hi, core).
Axes of the slice: x: 4, y: 4, z: 4 (z_hi: 2, z_lo: 2; z = z_hi * 2 + z_lo), core: 2. Of those that a mesh axis runs over, the one named last changes fastest.
Arguments:
- tile_values: bfloat16 [32, 4, 32, 1, 256, 256], P('blk', 'rep'), may hold values from -0.1875 to 0.1875
- tile_rows: int32 [32, 4, 32, 1], P('blk', 'rep'), may hold values from 0 to 1, as said below
- tile_cols: int32 [32, 4, 32, 1], P('blk', 'rep'), may hold values from 0 to 1
- tile_counts: int32 [32, 4, 32], P('blk', 'rep'), may hold values from 0 to 1, as said below
- grad_out: bfloat16 [16384, 512], P('blk'), may hold values from -6 to 6
- features: bfloat16 [16384, 512], P(('blk', 'rep')), may hold values from -0.125 to 0.125
- weight: bfloat16 [512, 512], replicated, may hold values from -0.25 to 0.25
Outputs:
- grad_features: float32 [16384, 512], P(('blk', 'rep'))
- grad_weight: float32 [512, 512], replicated
Inputs may be any that keep to these rules, and one draw needn't show every extreme that they name: `tile_counts`: every device has some column block with all 1 slots used. `tile_rows`: for each row block and column block, the slots of all devices of that row block lie at distinct tile positions.
All inputs are finite; a program needn't handle non-finite values.
Results may differ from a plain program's by a relative error of at most 0.0029.
Values may be sent and summed in bfloat16 or wider, within the bound.
A program may use at most 128 MiB of HBM per device.

v0:
```python
import jax
import jax.numpy as jnp
from jax import lax
from jax.sharding import PartitionSpec as P


def block_terms(values_here, selected, col_idx, count_here, per_row):
    product = jnp.einsum(
        "jsab,jsaf->jsbf", values_here, selected, preferred_element_type=jnp.float32
    )
    slot_iota = jnp.arange(values_here.shape[1])[None, :]
    valid = (slot_iota < count_here[:, None]).astype(jnp.float32)
    place = (col_idx[..., None] == jnp.arange(per_row)[None, None, :]).astype(jnp.float32) * valid[
        ..., None
    ]
    return jnp.einsum("jsc,jsbf->jcbf", place, product, precision=lax.Precision.HIGHEST)


def body(tile_values, tile_rows, tile_cols, tile_counts, grad_out, features, weight):
    values_here = tile_values[0, 0]
    row_idx = tile_rows[0, 0]
    col_idx = tile_cols[0, 0]
    count_here = tile_counts[0, 0]
    tile_side = values_here.shape[-1]
    blk_rows = grad_out.shape[0]
    width = grad_out.shape[1]
    per_row = blk_rows // tile_side
    g_flat = grad_out.reshape(per_row, tile_side, width)
    selected = g_flat[row_idx]
    term = block_terms(values_here, selected, col_idx, count_here, per_row)
    own_block = lax.psum_scatter(
        term.reshape(blk_rows * lax.axis_size("blk"), width), "blk", scatter_dimension=0, tiled=True
    )
    shared = lax.psum_scatter(own_block, "rep", scatter_dimension=0, tiled=True)
    rounded = shared.astype(jnp.bfloat16)
    grad_features = lax.dot_general(
        rounded, weight, (((1,), (1,)), ((), ())), preferred_element_type=jnp.float32
    )
    partial_weight = lax.dot_general(
        features, rounded, (((0,), (0,)), ((), ())), preferred_element_type=jnp.float32
    )
    grad_weight = lax.psum(partial_weight, ("blk", "rep"))
    return (grad_features, grad_weight)


def solution(mesh):
    placed = (
        P("blk", "rep", None, None, None, None),
        P("blk", "rep", None, None),
        P("blk", "rep", None, None),
        P("blk", "rep", None),
        P("blk", None),
        P(("blk", "rep"), None),
        P(),
    )
    return jax.shard_map(
        body, mesh=mesh, in_specs=placed, out_specs=(P(("blk", "rep"), None), P()), check_vma=False
    )
```

profile of v0, /device:TPU:1, one launch (start us, length us, event | category | flops | bytes accessed | tf_op | source)
XLA Modules:
  0.0 972.1 jit_solution(8976167498495208583)
XLA Ops:
  7.2 0.0 copy-start
  7.2 0.0 reduce-scatter.3.cloned.1.call-start
  7.2 0.7 fusion.6
  7.9 0.7 fusion.5
  8.6 0.0 copy-done
  8.6 4.9 gather_fusion
  13.5 12.7 %convolution_bitcast_fusion = f32[32,256,512]{1,2,0:T(8,128)} fusion(bf16[32,256,512]{2,1,0:T(8,128)(2,1)} %gather_fusion, bf16[1,1,32,1,256,256]{5,4,3,2,1,0:T(8,128)(2,1)} %param.7), kind=kOutput, calls=%fused_computation.2 | convolution fusion | flops 2147483648 | bytes 29360128 | tf_op jit(solution)/shard_map/jsab,jsaf->jsbf/dot_general | solution.py:8
  26.3 0.0 copy-start.4
  26.3 17.5 %copy.12 = f32[32,256,512]{2,1,0:T(8,128)} copy(f32[32,256,512]{1,2,0:T(8,128)} %convolution_bitcast_fusion) | data formatting | bytes 33554432 | tf_op jit(solution)/shard_map/jsab,jsaf->jsbf/dot_general | solution.py:8
  43.7 0.0 copy-done.4
  43.7 0.1 fusion.4
  43.8 19.0 %broadcast_multiply_fusion = f32[32,2,256,512]{3,2,1,0:T(8,128)} fusion(f32[32,256,512]{2,1,0:T(8,128)} %copy.12, f32[32,2]{1,0:T(8,128)S(1)} %fusion.4), kind=kLoop, calls=%fused_computation.1 | loop fusion | flops 8388608 | bytes 50331904 | tf_op jit(solution)/shard_map/jsc,jsbf->jcbf/dot_general | solution.py:16
  62.8 0.0 copy-start.3
  62.8 0.0 copy-start.2
  62.8 0.0 reduce-scatter.3.cloned.1.call-update
  62.8 0.0 copy-start.1
  62.8 0.0 reduce-scatter.5.cloned.1.call-start
  62.9 711.8 %reduce-scatter.3.cloned.1.call-done = f32[512,512]{1,0:T(8,128)} async-done(((f32[16384,512]{1,0:T(8,128)}), f32[512,512]{1,0:T(8,128)}) %reduce-scatter.3.cloned.1.call-update) | async-done | bytes 1048592 | tf_op jit(solution)/shard_map/reduce_scatter | solution.py:31
  774.7 0.0 reduce-scatter.5.cloned.1.call-update
  774.7 0.0 all-reduce.2.cloned.1.call-start
  774.8 35.5 %reduce-scatter.5.cloned.1.call-done = f32[128,512]{1,0:T(8,128)} async-done(((f32[512,512]{1,0:T(8,128)}), f32[128,512]{1,0:T(8,128)}) %reduce-scatter.5.cloned.1.call-update) | async-done | bytes 262160 | tf_op jit(solution)/shard_map/reduce_scatter | solution.py:34
  810.3 0.0 copy-done.3
  810.3 2.2 convolution_bitcast_fusion.1
  812.5 0.0 all-reduce.2.cloned.1.call-update
  812.5 0.0 copy-done.2
  812.5 2.0 fusion.2
  814.5 148.5 %all-reduce.2.cloned.1.call-done = f32[512,512]{0,1:T(8,128)} async-done(((f32[512,512]{0,1:T(8,128)}), f32[512,512]{0,1:T(8,128)}) %all-reduce.2.cloned.1.call-update) | async-done | bytes 1048592 | tf_op jit(solution)/shard_map/psum | solution.py:42
  963.0 2.5 copy.13
  965.5 0.0 copy-done.1
  (1 shorter events, 0.0 us)
Async XLA Ops:
  7.2 1.4 copy-start
  7.2 767.5 %reduce-scatter.3.cloned.1.call-start = ((), (), s32[]{:S(2)}) async-start(), calls=%async_computation.2 | async-start | bytes 34603008 | tf_op jit(solution)/shard_map/reduce_scatter | solution.py:31
  26.3 17.5 %copy-start.4 = (s32[1,1,32,1]{2,3,1,0:T(1,128)S(1)}, s32[1,1,32,1]{2,3,1,0:T(1,128)}, u32[]{:S(2)}) copy-start(s32[1,1,32,1]{2,3,1,0:T(1,128)} %param.9) | copy-start | bytes 388
  62.8 747.5 %copy-start.3 = (bf16[128,512]{1,0:T(8,128)(2,1)S(1)}, bf16[128,512]{1,0:T(8,128)(2,1)}, u32[]{:S(2)}) copy-start(bf16[128,512]{1,0:T(8,128)(2,1)} %param.12) | copy-start | bytes 393220
  62.8 749.7 %copy-start.2 = (bf16[512,512]{1,0:T(8,128)(2,1)S(1)}, bf16[512,512]{1,0:T(8,128)(2,1)}, u32[]{:S(2)}) copy-start(bf16[512,512]{1,0:T(8,128)(2,1)} %param.13) | copy-start | bytes 1572868
  62.8 902.7 %copy-start.1 = (bf16[512,512]{1,0:T(8,128)(2,1)S(1)}, bf16[512,512]{1,0:T(8,128)(2,1)}, u32[]{:S(2)}) copy-start(bf16[512,512]{1,0:T(8,128)(2,1)} %param.11) | copy-start | bytes 1572868
  62.8 747.4 %reduce-scatter.5.cloned.1.call-start = ((), (), s32[]{:S(2)}) async-start(), calls=%async_computation.3 | async-start | bytes 1310720 | tf_op jit(solution)/shard_map/reduce_scatter | solution.py:34
  774.7 188.2 %all-reduce.2.cloned.1.call-start = ((), (), s32[]{:S(2)}) async-start(), calls=%async_computation.4 | async-start | bytes 2097152 | tf_op jit(solution)/shard_map/psum | solution.py:42
Sparse Core Ops, SparseCore 0:
  63.0 711.7 reduce-scatter.2
  777.4 32.8 reduce-scatter.4
  816.4 146.5 all-reduce.1
where the time goes:
time: 973 us; the launch traced here: 972 us
  waiting for transfers between devices  896 us (92%)
  local copies, waits for them, and re-layouts  24.9 us (3%)
  other arithmetic  20.4 us (2%)
  matrix products  16.9 us (2%)
  between operations  13.8 us (1%)
    reduce_scatter x1, waiting for transfers between devices, body(): lax.psum_scatter(term.reshape(blk_rows * lax.axis_size('blk'), width), 'b...  712 us
    psum x1, waiting for transfers between devices, body(): grad_weight = lax.psum(partial_weight, ('blk', 'rep'))  149 us
    reduce_scatter x1, waiting for transfers between devices, body(): shared = lax.psum_scatter(own_block, 'rep', scatter_dimension=0, tiled=True)  35.5 us
  transfers between devices with their start and end apart: 3, of which 3 were waited for; matrix products, arithmetic and copies ran while one was open for 0% of the time, Pallas kernels for 0%

commit v1 on v0

--- a/solution.py
+++ b/solution.py
@@ -39,7 +39,10 @@
     partial_weight = lax.dot_general(
         features, rounded, (((0,), (0,)), ((), ())), preferred_element_type=jnp.float32
     )
-    grad_weight = lax.psum(partial_weight, ("blk", "rep"))
+    convert_the_roads = lambda values, row_axis, along_axis: jax.lax.psum(
+        jax.lax.psum(values, row_axis), along_axis
+    )
+    grad_weight = convert_the_roads(partial_weight, "blk", "rep")
     return (grad_features, grad_weight)
 
 

time: 973 us -> 1180 us (1.21)
  waiting for transfers between devices: 896 us -> 1100 us
    psum x1 -> x2, waiting for transfers between devices: 149 us -> 356 us  [the longest x1 288 us: body(): jax.lax.psum(values, row_axis)]
  transfers between devices with their start and end apart: 3 -> 4, of which waited for: 3 -> 4; matrix products, arithmetic and copies ran while one was open for 0% -> 0% of each run, Pallas kernels for 0% -> 0%
where the time goes in v1:
time: 1180 us
  waiting for transfers between devices  1100 us (93%)
  local copies, waits for them, and re-layouts  24.9 us (2%)
  other arithmetic  20.4 us (2%)
  matrix products  16.9 us (1%)
  between operations  13.8 us (1%)
    reduce_scatter x1, waiting for transfers between devices, body(): lax.psum_scatter(term.reshape(blk_rows * lax.axis_size('blk'), width), 'b...  712 us
    psum x1, waiting for transfers between devices, body(): jax.lax.psum(values, row_axis)  288 us
    psum x1, waiting for transfers between devices, body(): jax.lax.psum(jax.lax.psum(values, row_axis), along_axis)  67.9 us
    reduce_scatter x1, waiting for transfers between devices, body(): shared = lax.psum_scatter(own_block, 'rep', scatter_dimension=0, tiled=True)  35.5 us
  transfers between devices with their start and end apart: 4, of which 4 were waited for; matrix products, arithmetic and copies ran while one was open for 0% of the time, Pallas kernels for 0%

profile of v1, /device:TPU:1, one launch (start us, length us, event | category | flops | bytes accessed | tf_op | source)
XLA Modules:
  0.0 1179.1 jit_solution(17238405719259061459)
XLA Ops:
  7.2 0.0 copy-start
  7.2 0.0 reduce-scatter.3.cloned.1.call-start
  7.2 0.7 fusion.6
  7.9 0.7 fusion.5
  8.6 0.0 copy-done
  8.6 4.9 gather_fusion
  13.5 12.7 %convolution_bitcast_fusion = f32[32,256,512]{1,2,0:T(8,128)} fusion(bf16[32,256,512]{2,1,0:T(8,128)(2,1)} %gather_fusion, bf16[1,1,32,1,256,256]{5,4,3,2,1,0:T(8,128)(2,1)} %param.7), kind=kOutput, calls=%fused_computation.2 | convolution fusion | flops 2147483648 | bytes 29360128 | tf_op jit(solution)/shard_map/jsab,jsaf->jsbf/dot_general | solution.py:8
  26.3 0.0 copy-start.4
  26.3 17.5 %copy.12 = f32[32,256,512]{2,1,0:T(8,128)} copy(f32[32,256,512]{1,2,0:T(8,128)} %convolution_bitcast_fusion) | data formatting | bytes 33554432 | tf_op jit(solution)/shard_map/jsab,jsaf->jsbf/dot_general | solution.py:8
  43.7 0.0 copy-done.4
  43.7 0.1 fusion.4
  43.8 19.0 %broadcast_multiply_fusion = f32[32,2,256,512]{3,2,1,0:T(8,128)} fusion(f32[32,256,512]{2,1,0:T(8,128)} %copy.12, f32[32,2]{1,0:T(8,128)S(1)} %fusion.4), kind=kLoop, calls=%fused_computation.1 | loop fusion | flops 8388608 | bytes 50331904 | tf_op jit(solution)/shard_map/jsc,jsbf->jcbf/dot_general | solution.py:16
  62.8 0.0 copy-start.3
  62.8 0.0 copy-start.2
  62.8 0.0 reduce-scatter.3.cloned.1.call-update
  62.8 0.0 copy-start.1
  62.8 0.0 reduce-scatter.5.cloned.1.call-start
  62.9 711.8 %reduce-scatter.3.cloned.1.call-done = f32[512,512]{1,0:T(8,128)} async-done(((f32[16384,512]{1,0:T(8,128)}), f32[512,512]{1,0:T(8,128)}) %reduce-scatter.3.cloned.1.call-update) | async-done | bytes 1048592 | tf_op jit(solution)/shard_map/reduce_scatter | solution.py:31
  774.7 0.0 reduce-scatter.5.cloned.1.call-update
  774.7 0.0 all-reduce.3.cloned.1.call-start
  774.8 35.5 %reduce-scatter.5.cloned.1.call-done = f32[128,512]{1,0:T(8,128)} async-done(((f32[512,512]{1,0:T(8,128)}), f32[128,512]{1,0:T(8,128)}) %reduce-scatter.5.cloned.1.call-update) | async-done | bytes 262160 | tf_op jit(solution)/shard_map/reduce_scatter | solution.py:34
  810.3 0.0 copy-done.3
  810.3 2.2 convolution_bitcast_fusion.1
  812.5 0.0 all-reduce.3.cloned.1.call-update
  812.5 0.0 all-reduce.5.cloned.1.call-start
  812.6 287.6 %all-reduce.3.cloned.1.call-done = f32[512,512]{0,1:T(8,128)} async-done(((f32[512,512]{0,1:T(8,128)}), f32[512,512]{0,1:T(8,128)}) %all-reduce.3.cloned.1.call-update) | async-done | bytes 1048592 | tf_op jit(solution)/shard_map/psum | solution.py:43
  1100.2 0.0 all-reduce.5.cloned.1.call-update
  1100.2 0.0 copy-done.2
  1100.2 2.0 fusion.2
  1102.2 67.9 %all-reduce.5.cloned.1.call-done = f32[512,512]{0,1:T(8,128)} async-done(((f32[512,512]{0,1:T(8,128)}), f32[512,512]{0,1:T(8,128)}) %all-reduce.5.cloned.1.call-update) | async-done | bytes 1048592 | tf_op jit(solution)/shard_map/psum | solution.py:42
  1170.1 2.5 copy.13
  1172.6 0.0 copy-done.1
  (1 shorter events, 0.0 us)
Async XLA Ops:
  7.2 1.4 copy-start
  7.2 767.5 %reduce-scatter.3.cloned.1.call-start = ((), (), s32[]{:S(2)}) async-start(), calls=%async_computation.2 | async-start | bytes 34603008 | tf_op jit(solution)/shard_map/reduce_scatter | solution.py:31
  26.3 17.5 %copy-start.4 = (s32[1,1,32,1]{2,3,1,0:T(1,128)S(1)}, s32[1,1,32,1]{2,3,1,0:T(1,128)}, u32[]{:S(2)}) copy-start(s32[1,1,32,1]{2,3,1,0:T(1,128)} %param.9) | copy-start | bytes 388
  62.8 747.5 %copy-start.3 = (bf16[128,512]{1,0:T(8,128)(2,1)S(1)}, bf16[128,512]{1,0:T(8,128)(2,1)}, u32[]{:S(2)}) copy-start(bf16[128,512]{1,0:T(8,128)(2,1)} %param.12) | copy-start | bytes 393220
  62.8 1037.4 %copy-start.2 = (bf16[512,512]{1,0:T(8,128)(2,1)S(1)}, bf16[512,512]{1,0:T(8,128)(2,1)}, u32[]{:S(2)}) copy-start(bf16[512,512]{1,0:T(8,128)(2,1)} %param.13) | copy-start | bytes 1572868
  62.8 1109.8 %copy-start.1 = (bf16[512,512]{1,0:T(8,128)(2,1)S(1)}, bf16[512,512]{1,0:T(8,128)(2,1)}, u32[]{:S(2)}) copy-start(bf16[512,512]{1,0:T(8,128)(2,1)} %param.11) | copy-start | bytes 1572868
  62.8 747.4 %reduce-scatter.5.cloned.1.call-start = ((), (), s32[]{:S(2)}) async-start(), calls=%async_computation.3 | async-start | bytes 1310720 | tf_op jit(solution)/shard_map/reduce_scatter | solution.py:34
  774.7 325.5 %all-reduce.3.cloned.1.call-start = ((), (), s32[]{:S(2)}) async-start(), calls=%async_computation.4 | async-start | bytes 2097152 | tf_op jit(solution)/shard_map/psum | solution.py:43
  812.5 357.6 %all-reduce.5.cloned.1.call-start = ((), (), s32[]{:S(2)}) async-start(), calls=%async_computation.5 | async-start | bytes 2097152 | tf_op jit(solution)/shard_map/psum | solution.py:42
Sparse Core Ops, SparseCore 0:
  63.0 711.7 reduce-scatter.2
  777.4 32.8 reduce-scatter.4
  813.5 286.6 all-reduce.2
  1102.6 67.4 all-reduce.4
